TPU v7x, 512 devices: a whole 4x4x16 slice. The times are simulated.
512 devices in a mesh: dp: 32 (over z_lo, y), tensor: 16 (over z_hi, x, core).
Axes of the slice: x: 4, y: 4, z: 16 (z_hi: 2, z_lo: 8; z = z_hi * 8 + z_lo), core: 2. Of those that a mesh axis runs over, the one named last changes fastest.
Arguments:
- tokens: bfloat16 [16384, 3200], P(('dp', 'tensor')), may hold values from -32 to 32
- norm_gain: bfloat16 [3200], replicated, may hold values from 0.5 to 1.5
- qkv_weight: bfloat16 [3, 3200, 4096], P(None, 'dp', 'tensor'), may hold values from -0.037123106 to 0.037123106
- q_gain: float32 [4096], P('tensor'), may hold values from 1.5 to 5
- k_gain: float32 [4096], P('tensor'), may hold values from 1.5 to 5
- out_weight: bfloat16 [4096, 3200], P('tensor', 'dp'), may hold values from -0.21875 to 0.21875
- layer_scale: float32 [3200], replicated, may hold values from 0.5 to 2
Outputs:
- mixed: bfloat16 [16384, 3200], P(('dp', 'tensor'))
All inputs are finite; a program needn't handle non-finite values.
Results may differ from a plain program's by a relative error of at most 0.015.
Values may be sent and summed in bfloat16 or wider, within the bound.
A program may use at most 64 MiB of HBM per device.

v0:
```python
import jax
import jax.numpy as jnp
from jax import lax
from jax.sharding import PartitionSpec as P

D = 3200
HEADS = 25
HD = 128


epsilon = 1e-06


def normalize_rows(rows, gain):
    row_vals = rows.astype(jnp.float32)
    row_sums = jnp.sum(row_vals * row_vals, axis=1, keepdims=True)
    return (row_vals * lax.rsqrt(row_sums / D + epsilon) * gain.astype(jnp.float32)).astype(
        jnp.bfloat16
    )


def shards(tokens, norm_gain, qkv_weight, q_gain, k_gain, out_weight, layer_scale):
    whole_rows = lax.all_gather(tokens, "tensor", axis=0, tiled=True)
    normed = normalize_rows(whole_rows, norm_gain)
    tile_rows = normed.shape[0]
    columns = qkv_weight.shape[2]
    heads_here = columns // HD
    full_weight = lax.all_gather(qkv_weight, "dp", axis=1, tiled=True)
    projections = jnp.einsum("td,idc->itc", normed, full_weight, preferred_element_type=jnp.float32)
    head_ids = lax.axis_index("tensor") * heads_here + jnp.arange(columns) // HD
    keep = (head_ids < HEADS).astype(jnp.float32)
    queries = projections[0] * keep
    keys = projections[1] * keep
    values = projections[2] * keep
    query_sums, key_sums = lax.psum(
        (
            jnp.sum(queries * queries, axis=1, keepdims=True),
            jnp.sum(keys * keys, axis=1, keepdims=True),
        ),
        "tensor",
    )
    width = HEADS * HD
    query_normed = (queries * lax.rsqrt(query_sums / width + epsilon) * q_gain).astype(jnp.bfloat16)
    key_normed = (keys * lax.rsqrt(key_sums / width + epsilon) * k_gain).astype(jnp.bfloat16)
    value_rounded = values.astype(jnp.bfloat16)
    query_heads = query_normed.reshape(tile_rows, heads_here, HD)
    key_heads = key_normed.reshape(tile_rows, heads_here, HD)
    value_heads = value_rounded.reshape(tile_rows, heads_here, HD)
    scores = jnp.einsum(
        "qhd,khd->hqk", query_heads, key_heads, preferred_element_type=jnp.float32
    ) * HD ** (-0.5)
    probs = jax.nn.softmax(scores, axis=-1).astype(jnp.bfloat16)
    attended = jnp.einsum("hqk,khd->qhd", probs, value_heads, preferred_element_type=jnp.float32)
    attended = attended.astype(jnp.bfloat16).reshape(tile_rows, columns)
    terms = jnp.dot(
        attended,
        lax.all_gather(out_weight, "dp", axis=1, tiled=True),
        preferred_element_type=jnp.float32,
    )
    projected = lax.psum_scatter(
        terms.astype(jnp.bfloat16), "tensor", scatter_dimension=0, tiled=True
    ).astype(jnp.float32)
    return (tokens.astype(jnp.float32) + layer_scale * projected).astype(jnp.bfloat16)


def solution(mesh):
    placed = (
        P(("dp", "tensor"), None),
        P(),
        P(None, "dp", "tensor"),
        P("tensor"),
        P("tensor"),
        P("tensor", "dp"),
        P(),
    )
    return jax.shard_map(
        shards, mesh=mesh, in_specs=placed, out_specs=P(("dp", "tensor"), None), check_vma=False
    )
```

profile of v0, /device:TPU:1, one launch (start us, length us, event | category | flops | bytes accessed | tf_op | source)
XLA Modules:
  0.0 794.0 jit_solution(5194999881304023145)
XLA Ops:
  6.5 0.0 all-gather.9.cloned.1.call-start
  6.5 0.7 all-gather.9.cloned.1.call-update
  7.3 0.0 all-gather.5.cloned.1.call-start
  7.3 0.7 all-gather.5.cloned.1.call-update
  8.0 0.0 all-gather.7.cloned.1.call-start
  8.1 1.7 copy.14
  9.7 0.0 all-gather.7.cloned.1.call-update
  9.8 0.0 reduce-scatter.2.cloned.1.call-start
  9.8 0.7 convert_element_type.54
  10.5 206.5 %all-gather.9.cloned.1.call-done = bf16[32,100,256]{2,1,0:T(8,128)(2,1)} async-done(((bf16[1,100,256]{2,1,0:T(8,128)(2,1)}), bf16[32,100,256]{2,1,0:T(8,128)(2,1)}) %all-gather.9.cloned.1.call-update) | async-done | bytes 1638416 | tf_op jit(solution)/shard_map/all_gather | solution.py:57
  217.0 2.3 reshape.79
  219.3 129.0 %all-gather.5.cloned.1.call-done = bf16[512,3200]{1,0:T(8,128)(2,1)} async-done(((bf16[32,3200]{1,0:T(8,128)(2,1)}), bf16[512,3200]{1,0:T(8,128)(2,1)}) %all-gather.5.cloned.1.call-update) | async-done | bytes 3276816 | tf_op jit(solution)/shard_map/all_gather | solution.py:23
  348.3 2.6 fusion.1
  351.0 204.2 %all-gather.7.cloned.1.call-done = bf16[3,3200,256]{2,0,1:T(4,128)(2,1)} async-done(((bf16[3,100,256]{2,0,1:T(4,128)(2,1)}), bf16[3,3200,256]{2,0,1:T(4,128)(2,1)}) %all-gather.7.cloned.1.call-update) | async-done | bytes 4915216 | tf_op jit(solution)/shard_map/all_gather | solution.py:28
  555.1 6.4 fusion.11
  561.5 0.0 copy-start.2
  561.5 0.0 copy-start.3
  561.5 0.1 fusion.30
  561.7 0.2 fusion.20
  561.9 81.6 %all-reduce = (f32[512,1]{0,1:T(1,128)S(1)}, f32[512,1]{0,1:T(1,128)S(1)}) all-reduce(f32[512,1]{0,1:T(1,128)S(1)} %bitcast.42, f32[512,1]{0,1:T(1,128)S(1)} %bitcast.41), channel_id=1, replica_groups=mesh['dp'=32,'tensor'=16] {'tensor'}, use_global_device_ids=true, to_apply=%region_4.5 | all-reduce | flops 1024 | bytes 8192 | tf_op jit(solution)/shard_map/psum | solution.py:35
  643.5 0.0 copy-done.2
  643.5 0.0 copy-done.3
  643.5 2.3 fusion.31
  645.8 2.0 convolution_convert_fusion.1
  647.8 2.8 convolution_convert_fusion
  650.6 0.0 copy-start
  650.6 0.0 copy-start.1
  650.6 0.0 reduce-scatter.2.cloned.1.call-update
  650.6 135.2 %reduce-scatter.2.cloned.1.call-done = bf16[32,3200]{1,0:T(8,128)(2,1)} async-done(((bf16[512,3200]{1,0:T(8,128)(2,1)}), bf16[32,3200]{1,0:T(8,128)(2,1)}) %reduce-scatter.2.cloned.1.call-update) | async-done | bytes 204816 | tf_op jit(solution)/shard_map/reduce_scatter | solution.py:60
  785.8 0.0 copy-done
  785.8 0.0 copy-done.1
  785.8 1.7 add_convert_fusion
  (4 shorter events, 0.0 us)
Async XLA Ops:
  6.5 210.5 %all-gather.9.cloned.1.call-start = ((), (), s32[]{:S(2)}) async-start(), calls=%async_computation.4 | async-start | bytes 1757184 | tf_op jit(solution)/shard_map/all_gather | solution.py:57
  7.3 341.1 %all-gather.5.cloned.1.call-start = ((), (), s32[]{:S(2)}) async-start(), calls=%async_computation.1 | async-start | bytes 3481600 | tf_op jit(solution)/shard_map/all_gather | solution.py:23
  8.0 547.1 %all-gather.7.cloned.1.call-start = ((), (), s32[]{:S(2)}) async-start(), calls=%async_computation.2 | async-start | bytes 6758400 | tf_op jit(solution)/shard_map/all_gather | solution.py:28
  9.8 776.0 %reduce-scatter.2.cloned.1.call-start = ((), (), s32[]{:S(2)}) async-start(), calls=%async_computation.3 | async-start | bytes 3481600 | tf_op jit(solution)/shard_map/reduce_scatter | solution.py:60
  561.5 82.0 %copy-start.2 = (f32[256]{0:T(256)S(1)}, f32[256]{0:T(256)}, u32[]{:S(2)}) copy-start(f32[256]{0:T(256)} %param.11) | copy-start | bytes 3076
  561.5 82.0 %copy-start.3 = (f32[256]{0:T(256)S(1)}, f32[256]{0:T(256)}, u32[]{:S(2)}) copy-start(f32[256]{0:T(256)} %param.10) | copy-start | bytes 3076
  650.6 135.2 %copy-start = (bf16[32,3200]{1,0:T(8,128)(2,1)S(1)}, bf16[32,3200]{1,0:T(8,128)(2,1)}, u32[]{:S(2)}) copy-start(bf16[32,3200]{1,0:T(8,128)(2,1)} %param.7) | copy-start | bytes 614404
  650.6 135.2 %copy-start.1 = (f32[3200]{0:T(1024)S(1)}, f32[3200]{0:T(1024)}, u32[]{:S(2)}) copy-start(f32[3200]{0:T(1024)} %param.13) | copy-start | bytes 38404
Sparse Core Ops, SparseCore 0:
  9.4 207.5 all-gather.8
  220.3 127.9 all-gather.4
  350.4 204.6 all-gather.6
  650.7 135.0 reduce-scatter.1
where the time goes:
time: 795 us; the launch traced here: 794 us
  waiting for transfers between devices  676 us (85%)
  blocking collectives  81.6 us (10%)
  matrix products  13.4 us (2%)
  between operations  13.2 us (2%)
    all_gather x1, waiting for transfers between devices, shards(): lax.all_gather(out_weight, 'dp', axis=1, tiled=True)  206 us
    all_gather x1, waiting for transfers between devices, shards(): full_weight = lax.all_gather(qkv_weight, 'dp', axis=1, tiled=True)  204 us
    reduce_scatter x1, waiting for transfers between devices, shards(): lax.psum_scatter(terms.astype(jnp.bfloat16), 'tensor', scatter_dimension=...  135 us
    all_gather x1, waiting for transfers between devices, shards(): whole_rows = lax.all_gather(tokens, 'tensor', axis=0, tiled=True)  129 us
    psum x1, blocking collectives, shards(): lax.psum((jnp.sum(queries * queries, axis=1, keepdims=True), jnp.sum(keys...  81.6 us
  transfers between devices with their start and end apart: 4, of which 4 were waited for; matrix products, arithmetic and copies ran while one was open for 1% of the time, Pallas kernels for 0%

commit v1 on v0

v1 whole, which is shorter than its diff:
```python
import jax
import jax.numpy as jnp
from jax import lax
from jax.experimental import pallas as pl
from jax.experimental.pallas import tpu as pltpu
from jax.sharding import PartitionSpec as P

D = 3200
HEADS = 25
HD = 128
EPS = 1e-06
WIDTH = HEADS * HD
QKV_ROWS = 304
OUT_ROWS = 112
COLS = 640
CHUNKS = D // COLS
MESH = pl.DeviceIdType.MESH
F32 = jnp.float32
BF16 = jnp.bfloat16


def device(y, z, half, x, core):
    return (z * 4 + y, half * 8 + x * 2 + core)


def kernel(
    tok_ref, gain_ref, wa_ref, wb_ref, qg_ref, kg_ref, ls_ref, out_ref,
    xg, abuf, bbuf, wfull, ofull, qkf, heads, att, stage, srecv, szrecv, sown,
    terms, rs1, mid, rs2, wown, wsend, rs3,
    tok_recv, tok_send, w_recv, w_send, s_recv, s_send, r_recv, r_send,
):
    dp = lax.axis_index("dp")
    tensor = lax.axis_index("tensor")
    y, z = dp % 4, dp // 4
    half, x, core = tensor // 8, (tensor // 2) % 4, tensor % 2
    y_up, y_down, y_far = (y + 1) % 4, (y + 3) % 4, (y + 2) % 4
    sibling = device(y, z, half, x, 1 - core)
    across = device(y, z, 1 - half, x, core)

    def near(dx, other):
        c = (core + other) % 2
        return device(y, z, half, (x + dx) % 4, c)

    barrier = pltpu.get_barrier_semaphore()

    def greet(target):
        pl.semaphore_signal(barrier, 1, device_id=target, device_id_type=MESH)

    greet(device(y_up, z, half, x, core))
    greet(device(y_down, z, half, x, core))
    for dx in range(4):
        for other in range(2):
            if dx or other:
                greet(near(dx, other))
    greet(across)

    @pl.when(z > 0)
    def _():
        greet(device(y, z - 1, half, x, core))

    @pl.when(z < 7)
    def _():
        greet(device(y, z + 1, half, x, core))

    def remote(src, dst, send, recv, target):
        return pltpu.make_async_remote_copy(
            src_ref=src, dst_ref=dst, send_sem=send, recv_sem=recv,
            device_id=target, device_id_type=MESH,
        )

    def arrived(ref, sem):
        pltpu.make_async_copy(ref, ref, sem).wait()

    def row_block(h, xx, c):
        return pl.ds(pl.multiple_of(c * 256 + h * 128 + xx * 32, 32), 32)

    tok = tok_ref[...].astype(F32)
    sq = jnp.sum(tok * tok, axis=1, keepdims=True)
    xg[row_block(half, x, core), :] = (
        tok * lax.rsqrt(sq / D + EPS) * gain_ref[...].astype(F32)
    ).astype(BF16)
    mine = z * 4 + y
    abuf[mine] = wa_ref[...]
    bbuf[mine] = wb_ref[...]

    pl.semaphore_wait(
        barrier, 10 + (z > 0).astype(jnp.int32) + (z < 7).astype(jnp.int32)
    )

    def tok_copy(h, xx, c, target, slot):
        ref = xg.at[row_block(h, xx, c), :]
        return remote(
            ref, ref, tok_send.at[slot], tok_recv.at[h * 8 + xx * 2 + c], target
        )

    def tok_wait(h, xx, c):
        arrived(xg.at[row_block(h, xx, c), :], tok_recv.at[h * 8 + xx * 2 + c])

    def tok_spread(h, base):
        for dx in range(1, 4):
            tok_copy(h, x, core, near(dx, 0), base + dx - 1).start()
        tok_copy(h, x, core, sibling, base + 3).start()

    def tok_pass(h, base):
        for dx in range(1, 4):
            xx = (x + dx) % 4
            tok_wait(h, xx, core)
            tok_copy(h, xx, core, sibling, base + dx - 1).start()

    bufs = (abuf, bbuf)

    def z_send(cls, zs, dz, kind):
        b = zs * 4 + y
        ref = bufs[cls].at[b]
        return remote(
            ref, ref, w_send.at[cls, kind, zs], w_recv.at[cls, b, 0],
            device(y, z + dz, half, x, core),
        )

    def y_send(cls, zs, yt, kind):
        b = zs * 4 + y
        ref = bufs[cls].at[b]
        return remote(
            ref, ref, w_send.at[cls, kind, zs], w_recv.at[cls, b, 0],
            device(yt, z, half, x, core),
        )

    def y_pass(cls, zs, ysrc, yt, part, kind):
        b = zs * 4 + ysrc
        ref = bufs[cls].at[b, :, pl.ds(part * 128, 128)]
        return remote(
            ref, ref, w_send.at[cls, kind, zs], w_recv.at[cls, b, part],
            device(yt, z, half, x, core),
        )

    def send_y(cls, zs):
        y_send(cls, zs, y_up, 2).start()
        y_send(cls, zs, y_down, 3).start()

    def first_step(cls):
        @pl.when(z < 7)
        def _():
            z_send(cls, z, 1, 0).start()

        @pl.when(z > 0)
        def _():
            z_send(cls, z, -1, 1).start()

        send_y(cls, z)

    def step(cls, s):
        @pl.when(z >= s)
        def _():
            zs = z - s
            arrived(bufs[cls].at[zs * 4 + y], w_recv.at[cls, zs * 4 + y, 0])

            @pl.when(z < 7)
            def _():
                z_send(cls, zs, 1, 0).start()

            send_y(cls, zs)

        @pl.when(z + s <= 7)
        def _():
            zs = z + s
            arrived(bufs[cls].at[zs * 4 + y], w_recv.at[cls, zs * 4 + y, 0])

            @pl.when(z > 0)
            def _():
                z_send(cls, zs, -1, 1).start()

            send_y(cls, zs)

    def pass_one(cls, zs):
        arrived(bufs[cls].at[zs * 4 + y_down], w_recv.at[cls, zs * 4 + y_down, 0])
        y_pass(cls, zs, y_down, y_up, 0, 4).start()
        arrived(bufs[cls].at[zs * 4 + y_up], w_recv.at[cls, zs * 4 + y_up, 0])
        y_pass(cls, zs, y_up, y_down, 1, 5).start()

    def passes(cls, s):
        @pl.when(z >= s)
        def _():
            pass_one(cls, z - s)

        @pl.when((z + s <= 7) & (s > 0))
        def _():
            pass_one(cls, z + s)

    def finish(cls, zs):
        b = zs * 4 + y_far
        for part in range(2):
            arrived(
                bufs[cls].at[b, :, pl.ds(part * 128, 128)], w_recv.at[cls, b, part]
            )

    def sent(cls):
        @pl.loop(0, 8)
        def _(zs):
            @pl.when((z < 7) & (zs <= z))
            def _():
                z_send(cls, zs, 1, 0).wait_send()

            @pl.when((z > 0) & (zs >= z))
            def _():
                z_send(cls, zs, -1, 1).wait_send()

            y_send(cls, zs, y_up, 2).wait_send()
            y_send(cls, zs, y_down, 3).wait_send()
            y_pass(cls, zs, y_down, y_up, 0, 4).wait_send()
            y_pass(cls, zs, y_up, y_down, 1, 5).wait_send()

    tok_copy(half, x, core, across, 0).start()
    tok_spread(half, 1)
    first_step(0)

    @pl.loop(1, 4)
    def _(s):
        step(0, s)
        passes(0, s - 1)

    tok_pass(half, 5)

    @pl.loop(4, 8)
    def _(s):
        step(0, s)
        passes(0, s - 1)

    passes(0, 7)
    tok_wait(1 - half, x, core)
    tok_spread(1 - half, 8)
    first_step(1)

    @pl.loop(1, 8)
    def _(s):
        step(1, s)

    tok_pass(1 - half, 12)

    @pl.loop(0, 8)
    def _(zs):
        finish(0, zs)
        rows = pl.ds(pl.multiple_of(zs * 400, 16), 400)
        for i in range(3):
            wfull[i, rows, :] = jnp.concatenate(
                [abuf[zs * 4 + j, i * 100 : i * 100 + 100, :] for j in range(4)], axis=0
            )

    for h in range(2):
        for xx in range(4):
            tok_wait(h, xx, 1 - core)

    keep = (
        tensor * 2 + lax.broadcasted_iota(jnp.int32, (1, 256), 1) // HD < HEADS
    ).astype(F32)

    def project(i):
        return jnp.dot(xg[...], wfull[i], preferred_element_type=F32) * keep

    sums = []
    for i in range(2):
        qkf[i] = project(i)
        sums.append(jnp.sum(qkf[i] * qkf[i], axis=1, keepdims=True))
    lane = lax.broadcasted_iota(jnp.int32, (512, 128), 1)
    stage[...] = jnp.where(
        lane == 0, sums[0], jnp.where(lane == 1, sums[1], 0.0)
    ).T
    spot = x * 2 + core
    for i in range(2):
        for j in range(4):
            srecv[spot, pl.ds(i * 4 + j, 1), :] = stage[i : i + 1, j * 128 : j * 128 + 128]

    def sum_copy(dx, other):
        return remote(
            srecv.at[spot], srecv.at[spot], s_send.at[dx * 2 + other],
            s_recv.at[spot], near(dx, other),
        )

    for dx in range(4):
        for other in range(2):
            if dx or other:
                sum_copy(dx, other).start()

    heads[2] = project(2).astype(BF16)

    @pl.loop(0, 8)
    def _(s):
        passes(1, s)

    for dx in range(4):
        for other in range(2):
            if dx or other:
                other_spot = ((x + dx) % 4) * 2 + (core + other) % 2
                arrived(srecv.at[other_spot], s_recv.at[other_spot])
    total = srecv[0]
    for i in range(1, 8):
        total += srecv[i]
    sown[...] = total
    across_sum = remote(sown, szrecv, s_send.at[0], s_recv.at[8], across)
    for dx in range(4):
        for other in range(2):
            if dx or other:
                sum_copy(dx, other).wait_send()
    across_sum.start()

    @pl.loop(0, 8)
    def _(zs):
        finish(1, zs)
        ofull[pl.ds(pl.multiple_of(zs * 400, 16), 400), :] = jnp.concatenate(
            [bbuf[zs * 4 + j, 0:100, :] for j in range(4)], axis=0
        )

    across_sum.wait()
    total = sown[...] + szrecv[...]
    for i in range(2):
        for j in range(4):
            stage[i : i + 1, j * 128 : j * 128 + 128] = total[i * 4 + j : i * 4 + j + 1, :]
    columns = stage[...].T
    heads[0] = (
        qkf[0] * lax.rsqrt(columns[:, 0:1] / WIDTH + EPS) * qg_ref[...]
    ).astype(BF16)
    heads[1] = (
        qkf[1] * lax.rsqrt(columns[:, 1:2] / WIDTH + EPS) * kg_ref[...]
    ).astype(BF16)

    for h in range(2):
        cols = slice(h * HD, h * HD + HD)

        @pl.loop(0, 2)
        def _(r):
            rows = pl.ds(pl.multiple_of(r * 256, 256), 256)
            scores = lax.dot_general(
                heads[0, rows, cols], heads[1, :, cols], (((1,), (1,)), ((), ())),
                preferred_element_type=F32,
            ) * HD ** (-0.5)
            e = jnp.exp(scores - jnp.max(scores, axis=1, keepdims=True))
            probs = (e / jnp.sum(e, axis=1, keepdims=True)).astype(BF16)
            att[rows, cols] = jnp.dot(
                probs, heads[2, :, cols], preferred_element_type=F32
            ).astype(BF16)

    def to_sibling(c):
        return remote(
            terms.at[c, 1 - core], rs1.at[c], r_send.at[c, 0], r_recv.at[c, 0], sibling
        )

    def to_near(c, dx):
        return remote(
            mid.at[c, (x + dx) % 4], rs2.at[c, dx - 1], r_send.at[c, dx],
            r_recv.at[c, dx], near(dx, 0),
        )

    def to_across(c):
        return remote(wsend.at[c], rs3.at[c], r_send.at[c, 4], r_recv.at[c, 4], across)

    def stage_one(c):
        part = lax.dot_general(
            att[...], ofull[c * COLS : c * COLS + COLS, :], (((1,), (1,)), ((), ())),
            preferred_element_type=F32,
        )
        terms[c] = part.astype(BF16).reshape(2, 256, COLS)
        to_sibling(c).start()

    def stage_two(c):
        arrived(rs1.at[c], r_recv.at[c, 0])
        both = (terms[c, core].astype(F32) + rs1[c].astype(F32)).astype(BF16)
        both = both.reshape(2, 4, 32, COLS)
        for xx in range(4):
            for h in range(2):
                mid[c, xx, h] = both[h, xx]
        for dx in range(1, 4):
            to_near(c, dx).start()

    def stage_three(c):
        for dx in range(1, 4):
            arrived(rs2.at[c, dx - 1], r_recv.at[c, dx])

        def summed(h):
            s = mid[c, x, h].astype(F32)
            for dx in range(3):
                s += rs2[c, dx, h].astype(F32)
            return s

        wsend[c] = summed(1 - half).astype(BF16)
        to_across(c).start()
        wown[c] = summed(half)

    def stage_four(c):
        arrived(rs3.at[c], r_recv.at[c, 4])
        cols = slice(c * COLS, c * COLS + COLS)
        projected = wown[c] + rs3[c].astype(F32)
        out_ref[:, cols] = (
            tok_ref[:, cols].astype(F32) + ls_ref[:, cols] * projected
        ).astype(BF16)

    for t in range(CHUNKS + 3):
        if t < CHUNKS:
            stage_one(t)
        if 0 <= t - 1 < CHUNKS:
            stage_two(t - 1)
        if 0 <= t - 2 < CHUNKS:
            stage_three(t - 2)
    for c in range(CHUNKS):
        stage_four(c)

    for slot in range(15):
        tok_copy(half, x, core, sibling, slot).wait_send()
    sent(0)
    sent(1)
    for c in range(CHUNKS):
        to_sibling(c).wait_send()
        for dx in range(1, 4):
            to_near(c, dx).wait_send()
        to_across(c).wait_send()


def shards(tokens, norm_gain, qkv_weight, q_gain, k_gain, out_weight, layer_scale):
    wa = jnp.pad(qkv_weight.reshape(300, 256), ((0, QKV_ROWS - 300), (0, 0)))
    wb = jnp.pad(out_weight.T, ((0, OUT_ROWS - 100), (0, 0)))
    vmem = pl.BlockSpec(memory_space=pltpu.VMEM)
    dma = pltpu.SemaphoreType.DMA
    return pl.pallas_call(
        kernel,
        out_shape=jax.ShapeDtypeStruct((32, D), BF16),
        in_specs=[vmem] * 7,
        out_specs=vmem,
        scratch_shapes=[
            pltpu.VMEM((512, D), BF16),
            pltpu.VMEM((32, QKV_ROWS, 256), BF16),
            pltpu.VMEM((32, OUT_ROWS, 256), BF16),
            pltpu.VMEM((3, D, 256), BF16),
            pltpu.VMEM((D, 256), BF16),
            pltpu.VMEM((2, 512, 256), F32),
            pltpu.VMEM((3, 512, 256), BF16),
            pltpu.VMEM((512, 256), BF16),
            pltpu.VMEM((128, 512), F32),
            pltpu.VMEM((8, 8, 128), F32),
            pltpu.VMEM((8, 128), F32),
            pltpu.VMEM((8, 128), F32),
            pltpu.VMEM((CHUNKS, 2, 256, COLS), BF16),
            pltpu.VMEM((CHUNKS, 256, COLS), BF16),
            pltpu.VMEM((CHUNKS, 4, 2, 32, COLS), BF16),
            pltpu.VMEM((CHUNKS, 3, 2, 32, COLS), BF16),
            pltpu.VMEM((CHUNKS, 32, COLS), F32),
            pltpu.VMEM((CHUNKS, 32, COLS), BF16),
            pltpu.VMEM((CHUNKS, 32, COLS), BF16),
            dma((16,)),
            dma((15,)),
            dma((2, 32, 2)),
            dma((2, 6, 8)),
            dma((9,)),
            dma((8,)),
            dma((CHUNKS, 5)),
            dma((CHUNKS, 5)),
        ],
        compiler_params=pltpu.CompilerParams(
            collective_id=0, has_side_effects=True, vmem_limit_bytes=60 * 1024 * 1024
        ),
        cost_estimate=pl.CostEstimate(
            flops=4_000_000_000, bytes_accessed=1_000_000, transcendentals=600_000
        ),
    )(
        tokens, norm_gain.reshape(1, D), wa, wb, q_gain.reshape(1, 256),
        k_gain.reshape(1, 256), layer_scale.reshape(1, D),
    )


def solution(mesh):
    placed = (
        P(("dp", "tensor"), None),
        P(),
        P(None, "dp", "tensor"),
        P("tensor"),
        P("tensor"),
        P("tensor", "dp"),
        P(),
    )
    return jax.shard_map(
        shards, mesh=mesh, in_specs=placed, out_specs=P(("dp", "tensor"), None), check_vma=False
    )
```

time: 795 us -> 159 us (0.20)
  waiting for transfers between devices: 676 us -> 0 us
  Pallas kernels: 0 us -> 152 us
  blocking collectives: 81.6 us -> 0 us
  matrix products: 13.4 us -> 0 us
  between operations: 13.2 us -> 0.02 us
    all_gather x3 -> x0, waiting for transfers between devices: 540 us -> none  [the longest x1 206 us: shards(): lax.all_gather(out_weight, 'dp', axis=1, tiled=True)]
    pallas_call x0 -> x1, Pallas kernels: none -> 152 us  [shards(): pl.pallas_call(kernel, out_shape=jax.ShapeDtypeStruct((32, D), BF16), in_...]
    reduce_scatter x1 -> x0, waiting for transfers between devices: 135 us -> none  [shards(): lax.psum_scatter(terms.astype(jnp.bfloat16), 'tensor', scatter_dimension=...]
    psum x1 -> x0, blocking collectives: 81.6 us -> none  [shards(): lax.psum((jnp.sum(queries * queries, axis=1, keepdims=True), jnp.sum(keys...]
    dot_general x3 -> x0, matrix products: 11.1 us -> none  [the longest x1 6.38 us: shards(): jnp.einsum('td,idc->itc', normed, full_weight, preferred_element_type=jnp...]
  transfers between devices with their start and end apart: 4 -> 0, of which waited for: 4 -> 0; matrix products, arithmetic and copies ran while one was open for 1% -> 0% of each run, Pallas kernels for 0% -> 0%
where the time goes in v1:
time: 159 us; the launch traced here: 158 us
  Pallas kernels  152 us (96%)
  local copies, waits for them, and re-layouts  6.43 us (4%)
    pallas_call x1, Pallas kernels, shards(): pl.pallas_call(kernel, out_shape=jax.ShapeDtypeStruct((32, D), BF16), in_...  152 us

profile of v1, /device:TPU:1, one launch (start us, length us, event | category | flops | bytes accessed | tf_op | source)
XLA Modules:
  0.0 158.4 jit_solution(3386349033792959837)
XLA Ops:
  0.0 0.0 copy-start
  0.0 1.3 reshape.15.gain_ref
  1.3 1.3 reshape.19.ls_ref
  2.7 1.4 pad.9.wb_ref
  4.1 0.0 copy-done
  4.1 0.7 pad.8.wa_ref
  4.8 152.0 %shard_map.73 = bf16[32,3200]{1,0:T(8,128)(2,1)} custom-call(bf16[32,3200]{1,0:T(8,128)(2,1)} %tok_ref.1, bf16[1,3200]{1,0:T(2,128)(2,1)} %reshape.15.gain_ref, bf16[304,256]{1,0:T(8,128)(2,1)} %pad.8.wa_ref, bf16[112,256]{1,0:T(8,128)(2,1)} %pad.9.wb_ref, f32[1,256]{1,0:T(1,128)} %bitcast.4, f32[1,256]{1,0:T(1,128)} %bitcast.5, f32[1,3200]{1,0:T(1,128)} %reshape.19.ls_ref), custom_call_target="tpu_custom_call" | custom-call | flops 4000000000 | bytes 1000000 | tf_op jit(solution)/shard_map/pallas_call | solution.py:421
  156.8 1.6 %copy.9 = bf16[32,3200]{1,0:T(8,128)(2,1)} copy(bf16[32,3200]{1,0:T(8,128)(2,1)} %shard_map.73) | data formatting | bytes 409600
  (1 shorter events, 0.0 us)
Async XLA Ops:
  0.0 4.1 %copy-start = (bf16[3,100,256]{2,1,0:T(8,128)(2,1)S(1)}, bf16[3,100,256]{2,1,0:T(8,128)(2,1)}, u32[]{:S(2)}) copy-start(bf16[3,100,256]{2,1,0:T(8,128)(2,1)} %param.9) | copy-start | bytes 460804

commit v2 on v1

--- a/solution.py
+++ b/solution.py
@@ -24,7 +24,7 @@
 
 
 def kernel(
-    tok_ref, gain_ref, wa_ref, wb_ref, qg_ref, kg_ref, ls_ref, out_ref,
+    tok_ref, gain_ref, qkv_ref, o_ref, qg_ref, kg_ref, ls_ref, out_ref,
     xg, abuf, bbuf, wfull, ofull, qkf, heads, att, stage, srecv, szrecv, sown,
     terms, rs1, mid, rs2, wown, wsend, rs3,
     tok_recv, tok_send, w_recv, w_send, s_recv, s_send, r_recv, r_send,
@@ -46,13 +46,13 @@
     def greet(target):
         pl.semaphore_signal(barrier, 1, device_id=target, device_id_type=MESH)
 
+    greet(across)
     greet(device(y_up, z, half, x, core))
     greet(device(y_down, z, half, x, core))
     for dx in range(4):
         for other in range(2):
             if dx or other:
                 greet(near(dx, other))
-    greet(across)
 
     @pl.when(z > 0)
     def _():
@@ -71,111 +71,142 @@
     def arrived(ref, sem):
         pltpu.make_async_copy(ref, ref, sem).wait()
 
-    def row_block(h, xx, c):
-        return pl.ds(pl.multiple_of(c * 256 + h * 128 + xx * 32, 32), 32)
+    def row_block(h, xx, c, p):
+        return pl.ds(pl.multiple_of(c * 256 + h * 128 + xx * 32 + p * 16, 16), 16)
 
     tok = tok_ref[...].astype(F32)
     sq = jnp.sum(tok * tok, axis=1, keepdims=True)
-    xg[row_block(half, x, core), :] = (
-        tok * lax.rsqrt(sq / D + EPS) * gain_ref[...].astype(F32)
+    normed = (
+        tok * lax.rsqrt(sq / D + EPS) * gain_ref[...].astype(F32).reshape(1, D)
     ).astype(BF16)
+    for p in range(2):
+        xg[row_block(half, x, core, p), :] = normed[p * 16 : p * 16 + 16, :]
     mine = z * 4 + y
-    abuf[mine] = wa_ref[...]
-    bbuf[mine] = wb_ref[...]
+    for p in range(2):
+        cols = slice(p * 128, p * 128 + 128)
+        abuf[mine, p] = jnp.concatenate(
+            [qkv_ref[i, :, cols] for i in range(3)]
+            + [jnp.zeros((QKV_ROWS - 300, 128), BF16)],
+            axis=0,
+        )
+    for p in range(2):
+        bbuf[mine, p] = jnp.concatenate(
+            [
+                o_ref[:, p * 128 : p * 128 + 128],
+                jnp.zeros((OUT_ROWS - 100, 128), BF16),
+            ],
+            axis=0,
+        )
 
     pl.semaphore_wait(
         barrier, 10 + (z > 0).astype(jnp.int32) + (z < 7).astype(jnp.int32)
     )
 
-    def tok_copy(h, xx, c, target, slot):
-        ref = xg.at[row_block(h, xx, c), :]
+    def tok_copy(h, xx, c, p, target, slot):
+        ref = xg.at[row_block(h, xx, c, p), :]
         return remote(
-            ref, ref, tok_send.at[slot], tok_recv.at[h * 8 + xx * 2 + c], target
-        )
-
-    def tok_wait(h, xx, c):
-        arrived(xg.at[row_block(h, xx, c), :], tok_recv.at[h * 8 + xx * 2 + c])
-
-    def tok_spread(h, base):
-        for dx in range(1, 4):
-            tok_copy(h, x, core, near(dx, 0), base + dx - 1).start()
-        tok_copy(h, x, core, sibling, base + 3).start()
-
-    def tok_pass(h, base):
-        for dx in range(1, 4):
+            ref, ref, tok_send.at[slot, p], tok_recv.at[h * 8 + xx * 2 + c, p], target
+        )
+
+    def tok_wait(h, xx, c, p):
+        arrived(xg.at[row_block(h, xx, c, p), :], tok_recv.at[h * 8 + xx * 2 + c, p])
+
+    def tok_spread(h, p, base):
+        for dx in (2, 1, 3):
+            tok_copy(h, x, core, p, near(dx, 0), base + dx - 1).start()
+        tok_copy(h, x, core, p, sibling, base + 3).start()
+
+    def tok_pass(h, p, base):
+        for dx in (1, 3, 2):
             xx = (x + dx) % 4
-            tok_wait(h, xx, core)
-            tok_copy(h, xx, core, sibling, base + dx - 1).start()
+            tok_wait(h, xx, core, p)
+            tok_copy(h, xx, core, p, sibling, base + dx - 1).start()
 
     bufs = (abuf, bbuf)
 
-    def z_send(cls, zs, dz, kind):
-        b = zs * 4 + y
-        ref = bufs[cls].at[b]
+    def w_copy(cls, zs, yy, part, kind, target):
+        b = zs * 4 + yy
+        ref = bufs[cls].at[b, part]
         return remote(
-            ref, ref, w_send.at[cls, kind, zs], w_recv.at[cls, b, 0],
-            device(y, z + dz, half, x, core),
-        )
-
-    def y_send(cls, zs, yt, kind):
-        b = zs * 4 + y
-        ref = bufs[cls].at[b]
-        return remote(
-            ref, ref, w_send.at[cls, kind, zs], w_recv.at[cls, b, 0],
-            device(yt, z, half, x, core),
-        )
-
-    def y_pass(cls, zs, ysrc, yt, part, kind):
-        b = zs * 4 + ysrc
-        ref = bufs[cls].at[b, :, pl.ds(part * 128, 128)]
-        return remote(
-            ref, ref, w_send.at[cls, kind, zs], w_recv.at[cls, b, part],
-            device(yt, z, half, x, core),
-        )
+            ref, ref, w_send.at[cls, kind, zs, part], w_recv.at[cls, b, part], target
+        )
+
+    def w_wait(cls, zs, yy, part):
+        b = zs * 4 + yy
+        arrived(bufs[cls].at[b, part], w_recv.at[cls, b, part])
+
+    def z_right(cls, zs, part):
+        return w_copy(cls, zs, y, part, 0, device(y, z + 1, half, x, core))
+
+    def z_left(cls, zs, part):
+        return w_copy(cls, zs, y, part, 1, device(y, z - 1, half, x, core))
+
+    def y_plus(cls, zs, part):
+        return w_copy(cls, zs, y, part, 2, device(y_up, z, half, x, core))
+
+    def y_minus(cls, zs, part):
+        return w_copy(cls, zs, y, part, 3, device(y_down, z, half, x, core))
+
+    def pass_plus(cls, zs):
+        return w_copy(cls, zs, y_down, 0, 4, device(y_up, z, half, x, core))
+
+    def pass_minus(cls, zs):
+        return w_copy(cls, zs, y_up, 1, 5, device(y_down, z, half, x, core))
 
     def send_y(cls, zs):
-        y_send(cls, zs, y_up, 2).start()
-        y_send(cls, zs, y_down, 3).start()
-
-    def first_step(cls):
-        @pl.when(z < 7)
-        def _():
-            z_send(cls, z, 1, 0).start()
-
-        @pl.when(z > 0)
-        def _():
-            z_send(cls, z, -1, 1).start()
-
-        send_y(cls, z)
-
-    def step(cls, s):
-        @pl.when(z >= s)
-        def _():
-            zs = z - s
-            arrived(bufs[cls].at[zs * 4 + y], w_recv.at[cls, zs * 4 + y, 0])
+        y_plus(cls, zs, 0).start()
+        y_minus(cls, zs, 1).start()
+        y_plus(cls, zs, 1).start()
+        y_minus(cls, zs, 0).start()
+
+    def first_step(cls, spread):
+        for part in range(2):
 
             @pl.when(z < 7)
             def _():
-                z_send(cls, zs, 1, 0).start()
-
-            send_y(cls, zs)
-
-        @pl.when(z + s <= 7)
-        def _():
-            zs = z + s
-            arrived(bufs[cls].at[zs * 4 + y], w_recv.at[cls, zs * 4 + y, 0])
+                z_right(cls, z, part).start()
 
             @pl.when(z > 0)
             def _():
-                z_send(cls, zs, -1, 1).start()
-
-            send_y(cls, zs)
+                z_left(cls, z, part).start()
+
+        if spread:
+            send_y(cls, z)
+
+    def step(cls, s, spread):
+        for part in range(2):
+
+            @pl.when(z >= s)
+            def _():
+                w_wait(cls, z - s, y, part)
+
+                @pl.when(z < 7)
+                def _():
+                    z_right(cls, z - s, part).start()
+
+            @pl.when(z + s <= 7)
+            def _():
+                w_wait(cls, z + s, y, part)
+
+                @pl.when(z > 0)
+                def _():
+                    z_left(cls, z + s, part).start()
+
+        if spread:
+
+            @pl.when(z >= s)
+            def _():
+                send_y(cls, z - s)
+
+            @pl.when(z + s <= 7)
+            def _():
+                send_y(cls, z + s)
 
     def pass_one(cls, zs):
-        arrived(bufs[cls].at[zs * 4 + y_down], w_recv.at[cls, zs * 4 + y_down, 0])
-        y_pass(cls, zs, y_down, y_up, 0, 4).start()
-        arrived(bufs[cls].at[zs * 4 + y_up], w_recv.at[cls, zs * 4 + y_up, 0])
-        y_pass(cls, zs, y_up, y_down, 1, 5).start()
+        w_wait(cls, zs, y_down, 0)
+        pass_plus(cls, zs).start()
+        w_wait(cls, zs, y_up, 1)
+        pass_minus(cls, zs).start()
 
     def passes(cls, s):
         @pl.when(z >= s)
@@ -187,67 +218,92 @@
             pass_one(cls, z + s)
 
     def finish(cls, zs):
-        b = zs * 4 + y_far
+        w_wait(cls, zs, y_down, 1)
+        w_wait(cls, zs, y_up, 0)
         for part in range(2):
-            arrived(
-                bufs[cls].at[b, :, pl.ds(part * 128, 128)], w_recv.at[cls, b, part]
-            )
+            w_wait(cls, zs, y_far, part)
 
     def sent(cls):
         @pl.loop(0, 8)
         def _(zs):
-            @pl.when((z < 7) & (zs <= z))
-            def _():
-                z_send(cls, zs, 1, 0).wait_send()
-
-            @pl.when((z > 0) & (zs >= z))
-            def _():
-                z_send(cls, zs, -1, 1).wait_send()
-
-            y_send(cls, zs, y_up, 2).wait_send()
-            y_send(cls, zs, y_down, 3).wait_send()
-            y_pass(cls, zs, y_down, y_up, 0, 4).wait_send()
-            y_pass(cls, zs, y_up, y_down, 1, 5).wait_send()
-
-    tok_copy(half, x, core, across, 0).start()
-    tok_spread(half, 1)
-    first_step(0)
-
-    @pl.loop(1, 4)
+            for part in range(2):
+
+                @pl.when((z < 7) & (zs <= z))
+                def _():
+                    z_right(cls, zs, part).wait_send()
+
+                @pl.when((z > 0) & (zs >= z))
+                def _():
+                    z_left(cls, zs, part).wait_send()
+
+                y_plus(cls, zs, part).wait_send()
+                y_minus(cls, zs, part).wait_send()
+            pass_plus(cls, zs).wait_send()
+            pass_minus(cls, zs).wait_send()
+
+    for p in range(2):
+        tok_copy(half, x, core, p, across, 0).start()
+    first_step(0, True)
+    for p in range(2):
+        tok_spread(half, p, 1)
+
+    @pl.loop(1, 3)
     def _(s):
-        step(0, s)
-        passes(0, s - 1)
-
-    tok_pass(half, 5)
-
-    @pl.loop(4, 8)
+        step(0, s, True)
+
+    step(0, 3, True)
+    passes(0, 0)
+    for p in range(2):
+        tok_pass(half, p, 5)
+    tok_wait(1 - half, x, core, 0)
+    tok_spread(1 - half, 0, 8)
+    step(0, 4, True)
+    passes(0, 1)
+    tok_wait(1 - half, x, core, 1)
+    tok_spread(1 - half, 1, 8)
+    first_step(1, False)
+
+    @pl.loop(5, 8)
     def _(s):
-        step(0, s)
-        passes(0, s - 1)
-
-    passes(0, 7)
-    tok_wait(1 - half, x, core)
-    tok_spread(1 - half, 8)
-    first_step(1)
-
-    @pl.loop(1, 8)
+        step(0, s, True)
+        passes(0, s - 3)
+        step(1, s - 4, False)
+
+    for p in range(2):
+        tok_pass(1 - half, p, 12)
+
+    @pl.loop(5, 8)
     def _(s):
-        step(1, s)
-
-    tok_pass(1 - half, 12)
+        passes(0, s)
+        step(1, s - 1, False)
+
+    step(1, 7, False)
+
+    @pl.loop(0, 8)
+    def _(s):
+        @pl.when(z >= s)
+        def _():
+            send_y(1, z - s)
+
+        @pl.when((z + s <= 7) & (s > 0))
+        def _():
+            send_y(1, z + s)
 
     @pl.loop(0, 8)
     def _(zs):
         finish(0, zs)
         rows = pl.ds(pl.multiple_of(zs * 400, 16), 400)
         for i in range(3):
-            wfull[i, rows, :] = jnp.concatenate(
-                [abuf[zs * 4 + j, i * 100 : i * 100 + 100, :] for j in range(4)], axis=0
-            )
+            for p in range(2):
+                wfull[i, rows, p * 128 : p * 128 + 128] = jnp.concatenate(
+                    [abuf[zs * 4 + j, p, i * 100 : i * 100 + 100, :] for j in range(4)],
+                    axis=0,
+                )
 
     for h in range(2):
         for xx in range(4):
-            tok_wait(h, xx, 1 - core)
+            for p in range(2):
+                tok_wait(h, xx, 1 - core, p)
 
     keep = (
         tensor * 2 + lax.broadcasted_iota(jnp.int32, (1, 256), 1) // HD < HEADS
@@ -282,7 +338,7 @@
 
     heads[2] = project(2).astype(BF16)
 
-    @pl.loop(0, 8)
+    @pl.loop(0, 4)
     def _(s):
         passes(1, s)
 
@@ -302,12 +358,9 @@
                 sum_copy(dx, other).wait_send()
     across_sum.start()
 
-    @pl.loop(0, 8)
-    def _(zs):
-        finish(1, zs)
-        ofull[pl.ds(pl.multiple_of(zs * 400, 16), 400), :] = jnp.concatenate(
-            [bbuf[zs * 4 + j, 0:100, :] for j in range(4)], axis=0
-        )
+    @pl.loop(4, 8)
+    def _(s):
+        passes(1, s)
 
     across_sum.wait()
     total = sown[...] + szrecv[...]
@@ -316,10 +369,10 @@
             stage[i : i + 1, j * 128 : j * 128 + 128] = total[i * 4 + j : i * 4 + j + 1, :]
     columns = stage[...].T
     heads[0] = (
-        qkf[0] * lax.rsqrt(columns[:, 0:1] / WIDTH + EPS) * qg_ref[...]
+        qkf[0] * lax.rsqrt(columns[:, 0:1] / WIDTH + EPS) * qg_ref[...].reshape(1, 256)
     ).astype(BF16)
     heads[1] = (
-        qkf[1] * lax.rsqrt(columns[:, 1:2] / WIDTH + EPS) * kg_ref[...]
+        qkf[1] * lax.rsqrt(columns[:, 1:2] / WIDTH + EPS) * kg_ref[...].reshape(1, 256)
     ).astype(BF16)
 
     for h in range(2):
@@ -338,6 +391,20 @@
                 probs, heads[2, :, cols], preferred_element_type=F32
             ).astype(BF16)
 
+    for slot in range(15):
+        for p in range(2):
+            tok_copy(half, x, core, p, sibling, slot).wait_send()
+    sent(0)
+
+    @pl.loop(0, 8)
+    def _(zs):
+        finish(1, zs)
+        rows = pl.ds(pl.multiple_of(zs * 400, 16), 400)
+        for p in range(2):
+            ofull[rows, p * 128 : p * 128 + 128] = jnp.concatenate(
+                [bbuf[zs * 4 + j, p, 0:100, :] for j in range(4)], axis=0
+            )
+
     def to_sibling(c):
         return remote(
             terms.at[c, 1 - core], rs1.at[c], r_send.at[c, 0], r_recv.at[c, 0], sibling
@@ -384,12 +451,14 @@
         to_across(c).start()
         wown[c] = summed(half)
 
+    scale = ls_ref[...].reshape(1, D)
+
     def stage_four(c):
         arrived(rs3.at[c], r_recv.at[c, 4])
         cols = slice(c * COLS, c * COLS + COLS)
         projected = wown[c] + rs3[c].astype(F32)
         out_ref[:, cols] = (
-            tok_ref[:, cols].astype(F32) + ls_ref[:, cols] * projected
+            tok_ref[:, cols].astype(F32) + scale[:, cols] * projected
         ).astype(BF16)
 
     for t in range(CHUNKS + 3):
@@ -402,9 +471,6 @@
     for c in range(CHUNKS):
         stage_four(c)
 
-    for slot in range(15):
-        tok_copy(half, x, core, sibling, slot).wait_send()
-    sent(0)
     sent(1)
     for c in range(CHUNKS):
         to_sibling(c).wait_send()
@@ -414,8 +480,6 @@
 
 
 def shards(tokens, norm_gain, qkv_weight, q_gain, k_gain, out_weight, layer_scale):
-    wa = jnp.pad(qkv_weight.reshape(300, 256), ((0, QKV_ROWS - 300), (0, 0)))
-    wb = jnp.pad(out_weight.T, ((0, OUT_ROWS - 100), (0, 0)))
     vmem = pl.BlockSpec(memory_space=pltpu.VMEM)
     dma = pltpu.SemaphoreType.DMA
     return pl.pallas_call(
@@ -425,8 +489,8 @@
         out_specs=vmem,
         scratch_shapes=[
             pltpu.VMEM((512, D), BF16),
-            pltpu.VMEM((32, QKV_ROWS, 256), BF16),
-            pltpu.VMEM((32, OUT_ROWS, 256), BF16),
+            pltpu.VMEM((32, 2, QKV_ROWS, 128), BF16),
+            pltpu.VMEM((32, 2, OUT_ROWS, 128), BF16),
             pltpu.VMEM((3, D, 256), BF16),
             pltpu.VMEM((D, 256), BF16),
             pltpu.VMEM((2, 512, 256), F32),
@@ -443,10 +507,10 @@
             pltpu.VMEM((CHUNKS, 32, COLS), F32),
             pltpu.VMEM((CHUNKS, 32, COLS), BF16),
             pltpu.VMEM((CHUNKS, 32, COLS), BF16),
-            dma((16,)),
-            dma((15,)),
+            dma((16, 2)),
+            dma((15, 2)),
             dma((2, 32, 2)),
-            dma((2, 6, 8)),
+            dma((2, 6, 8, 2)),
             dma((9,)),
             dma((8,)),
             dma((CHUNKS, 5)),
@@ -459,8 +523,7 @@
             flops=4_000_000_000, bytes_accessed=1_000_000, transcendentals=600_000
         ),
     )(
-        tokens, norm_gain.reshape(1, D), wa, wb, q_gain.reshape(1, 256),
-        k_gain.reshape(1, 256), layer_scale.reshape(1, D),
+        tokens, norm_gain, qkv_weight, out_weight.T, q_gain, k_gain, layer_scale
     )
 
 

time: 159 us -> 137 us (0.86)
  Pallas kernels: 152 us -> 134 us
  local copies, waits for them, and re-layouts: 6.43 us -> 1.62 us
    pallas_call x1, Pallas kernels: 152 us -> 134 us  [shards(): pl.pallas_call(kernel, out_shape=jax.ShapeDtypeStruct((32, D), BF16), in_...]
    reshape x3 -> x0, local copies, waits for them, and re-layouts: 2.69 us -> none  [the longest x1 1.34 us: shards(): norm_gain.reshape(1, D)]
    pad x2 -> x0, local copies, waits for them, and re-layouts: 2.11 us -> none  [the longest x1 1.44 us: shards(): wb = jnp.pad(out_weight.T, ((0, OUT_ROWS - 100), (0, 0)))]
where the time goes in v2:
time: 137 us; the launch traced here: 136 us
  Pallas kernels  134 us (98%)
  local copies, waits for them, and re-layouts  1.62 us (1%)
    pallas_call x1, Pallas kernels, shards(): pl.pallas_call(kernel, out_shape=jax.ShapeDtypeStruct((32, D), BF16), in_...  134 us

profile of v2, /device:TPU:1, one launch (start us, length us, event | category | flops | bytes accessed | tf_op | source)
XLA Modules:
  0.0 135.7 jit_solution(5562061029055737221)
XLA Ops:
  0.0 134.1 %shard_map.73 = bf16[32,3200]{1,0:T(8,128)(2,1)} custom-call(bf16[32,3200]{1,0:T(8,128)(2,1)} %tok_ref.1, bf16[3200]{0:T(1024)(128)(2,1)} %gain_ref.1, bf16[3,100,256]{2,1,0:T(8,128)(2,1)} %qkv_ref.1, bf16[100,256]{1,0:T(8,128)(2,1)} %bitcast.1, f32[256]{0:T(256)} %qg_ref.1, f32[256]{0:T(256)} %kg_ref.1, f32[3200]{0:T(1024)} %ls_ref.1), custom_call_target="tpu_custom_call" | custom-call | flops 4000000000 | bytes 1000000 | tf_op jit(solution)/shard_map/pallas_call | solution.py:485
  134.1 1.6 %copy.9 = bf16[32,3200]{1,0:T(8,128)(2,1)} copy(bf16[32,3200]{1,0:T(8,128)(2,1)} %shard_map.73) | data formatting | bytes 409600

commit v3 on v2

--- a/solution.py
+++ b/solution.py
@@ -12,8 +12,9 @@
 WIDTH = HEADS * HD
 QKV_ROWS = 304
 OUT_ROWS = 112
-COLS = 640
-CHUNKS = D // COLS
+COLS = (256, 512, 512, 640, 512, 512, 256)
+CHUNKS = len(COLS)
+STARTS = tuple(sum(COLS[:c]) for c in range(CHUNKS))
 MESH = pl.DeviceIdType.MESH
 F32 = jnp.float32
 BF16 = jnp.bfloat16
@@ -23,12 +24,15 @@
     return (z * 4 + y, half * 8 + x * 2 + core)
 
 
-def kernel(
-    tok_ref, gain_ref, qkv_ref, o_ref, qg_ref, kg_ref, ls_ref, out_ref,
-    xg, abuf, bbuf, wfull, ofull, qkf, heads, att, stage, srecv, szrecv, sown,
-    terms, rs1, mid, rs2, wown, wsend, rs3,
-    tok_recv, tok_send, w_recv, w_send, s_recv, s_send, r_recv, r_send,
-):
+def kernel(*refs):
+    tok_ref, gain_ref, qkv_ref, o_ref, qg_ref, kg_ref, ls_ref, out_ref = refs[:8]
+    xg, abuf, bbuf, wfull, ofull, qkf, heads, att, stage, srecv, szrecv, sown = refs[8:20]
+    chunk_refs = refs[20:-10]
+    terms, rs1, mid, far, added, rs2, wown, wsend, rs3 = [
+        chunk_refs[i * CHUNKS : (i + 1) * CHUNKS] for i in range(9)
+    ]
+    tok_recv, tok_send, z8_recv, z8_send, w_recv, w_send = refs[-10:-4]
+    s_recv, s_send, r_recv, r_send = refs[-4:]
     dp = lax.axis_index("dp")
     tensor = lax.axis_index("tensor")
     y, z = dp % 4, dp // 4
@@ -122,6 +126,15 @@
             tok_wait(h, xx, core, p)
             tok_copy(h, xx, core, p, sibling, base + dx - 1).start()
 
+
+    def z8_copy(k):
+        ref = xg.at[pl.ds(pl.multiple_of(core * 256 + half * 128 + x * 32, 32), 32), pl.ds(k * 640, 640)]
+        return remote(ref, ref, z8_send.at[k], z8_recv.at[k], across)
+
+    def z8_wait(k):
+        ref = xg.at[pl.ds(pl.multiple_of(core * 256 + (1 - half) * 128 + x * 32, 32), 32), pl.ds(k * 640, 640)]
+        arrived(ref, z8_recv.at[k])
+
     bufs = (abuf, bbuf)
 
     def w_copy(cls, zs, yy, part, kind, target):
@@ -241,44 +254,45 @@
             pass_plus(cls, zs).wait_send()
             pass_minus(cls, zs).wait_send()
 
-    for p in range(2):
-        tok_copy(half, x, core, p, across, 0).start()
     first_step(0, True)
     for p in range(2):
         tok_spread(half, p, 1)
-
-    @pl.loop(1, 3)
-    def _(s):
-        step(0, s, True)
-
+    z8_copy(0).start()
+    step(0, 1, True)
+    z8_copy(1).start()
+    step(0, 2, True)
+    z8_copy(2).start()
+    passes(0, 0)
     step(0, 3, True)
-    passes(0, 0)
+    z8_copy(3).start()
+    passes(0, 1)
     for p in range(2):
         tok_pass(half, p, 5)
-    tok_wait(1 - half, x, core, 0)
-    tok_spread(1 - half, 0, 8)
     step(0, 4, True)
-    passes(0, 1)
-    tok_wait(1 - half, x, core, 1)
-    tok_spread(1 - half, 1, 8)
+    z8_copy(4).start()
     first_step(1, False)
-
-    @pl.loop(5, 8)
-    def _(s):
-        step(0, s, True)
-        passes(0, s - 3)
-        step(1, s - 4, False)
-
+    passes(0, 2)
+    step(0, 5, True)
+    step(1, 1, False)
+    passes(0, 3)
+    step(0, 6, True)
+    step(1, 2, False)
+    for k in range(5):
+        z8_wait(k)
     for p in range(2):
-        tok_pass(1 - half, p, 12)
-
-    @pl.loop(5, 8)
-    def _(s):
-        passes(0, s)
-        step(1, s - 1, False)
-
+        tok_spread(1 - half, p, 8)
+    passes(0, 4)
+    step(0, 7, True)
+    step(1, 3, False)
+    passes(0, 5)
+    step(1, 4, False)
+    passes(0, 6)
+    step(1, 5, False)
+    passes(0, 7)
+    step(1, 6, False)
+    tok_pass(1 - half, 0, 12)
+    tok_pass(1 - half, 1, 12)
     step(1, 7, False)
-
     @pl.loop(0, 8)
     def _(s):
         @pl.when(z >= s)
@@ -288,6 +302,7 @@
         @pl.when((z + s <= 7) & (s > 0))
         def _():
             send_y(1, z + s)
+
 
     @pl.loop(0, 8)
     def _(zs):
@@ -391,7 +406,9 @@
                 probs, heads[2, :, cols], preferred_element_type=F32
             ).astype(BF16)
 
-    for slot in range(15):
+    for k in range(5):
+        z8_copy(k).wait_send()
+    for slot in range(1, 15):
         for p in range(2):
             tok_copy(half, x, core, p, sibling, slot).wait_send()
     sent(0)
@@ -405,58 +422,82 @@
                 [bbuf[zs * 4 + j, p, 0:100, :] for j in range(4)], axis=0
             )
 
+    x_up, x_down, x_far = (x + 1) % 4, (x + 3) % 4, (x + 2) % 4
+
     def to_sibling(c):
         return remote(
-            terms.at[c, 1 - core], rs1.at[c], r_send.at[c, 0], r_recv.at[c, 0], sibling
-        )
-
-    def to_near(c, dx):
-        return remote(
-            mid.at[c, (x + dx) % 4], rs2.at[c, dx - 1], r_send.at[c, dx],
-            r_recv.at[c, dx], near(dx, 0),
+            terms[c].at[1 - core], rs1[c], r_send.at[c, 0], r_recv.at[c, 0], sibling
+        )
+
+    def far_copy(c, h):
+        return remote(
+            mid[c].at[x_far, h], far[c].at[h], r_send.at[c, 1 + h], r_recv.at[c, 1 + h],
+            near(3 if h else 1, 0),
+        )
+
+    def plain_copy(c, h):
+        return remote(
+            mid[c].at[x_down if h == 0 else x_up, h], rs2[c].at[1 - h, h],
+            r_send.at[c, 3 + h], r_recv.at[c, 3 + h], near(1 if h else 3, 0),
+        )
+
+    def added_copy(c, h):
+        return remote(
+            added[c].at[h], rs2[c].at[h, h], r_send.at[c, 5 + h], r_recv.at[c, 5 + h],
+            near(3 if h else 1, 0),
         )
 
     def to_across(c):
-        return remote(wsend.at[c], rs3.at[c], r_send.at[c, 4], r_recv.at[c, 4], across)
+        return remote(wsend[c], rs3[c], r_send.at[c, 7], r_recv.at[c, 7], across)
 
     def stage_one(c):
         part = lax.dot_general(
-            att[...], ofull[c * COLS : c * COLS + COLS, :], (((1,), (1,)), ((), ())),
+            att[...], ofull[STARTS[c] : STARTS[c] + COLS[c], :], (((1,), (1,)), ((), ())),
             preferred_element_type=F32,
         )
-        terms[c] = part.astype(BF16).reshape(2, 256, COLS)
+        terms[c][...] = part.astype(BF16).reshape(2, 256, COLS[c])
         to_sibling(c).start()
 
     def stage_two(c):
-        arrived(rs1.at[c], r_recv.at[c, 0])
-        both = (terms[c, core].astype(F32) + rs1[c].astype(F32)).astype(BF16)
-        both = both.reshape(2, 4, 32, COLS)
+        to_sibling(c).wait_recv()
+        both = (terms[c][core].astype(F32) + rs1[c][...].astype(F32)).astype(BF16)
+        both = both.reshape(2, 4, 32, COLS[c])
         for xx in range(4):
             for h in range(2):
-                mid[c, xx, h] = both[h, xx]
-        for dx in range(1, 4):
-            to_near(c, dx).start()
+                mid[c][xx, h] = both[h, xx]
+        for h in range(2):
+            far_copy(c, h).start()
+        for h in range(2):
+            plain_copy(c, h).start()
+
+    def stage_relay(c):
+        for h in range(2):
+            far_copy(c, h).wait_recv()
+            mine_too = mid[c][x_down if h else x_up, h].astype(F32)
+            added[c][h] = (mine_too + far[c][h].astype(F32)).astype(BF16)
+            added_copy(c, h).start()
 
     def stage_three(c):
-        for dx in range(1, 4):
-            arrived(rs2.at[c, dx - 1], r_recv.at[c, dx])
+        for h in range(2):
+            plain_copy(c, h).wait_recv()
+            added_copy(c, h).wait_recv()
 
         def summed(h):
-            s = mid[c, x, h].astype(F32)
-            for dx in range(3):
-                s += rs2[c, dx, h].astype(F32)
+            s = mid[c][x, h].astype(F32)
+            for side in range(2):
+                s += rs2[c][side, h].astype(F32)
             return s
 
-        wsend[c] = summed(1 - half).astype(BF16)
+        wsend[c][...] = summed(1 - half).astype(BF16)
         to_across(c).start()
-        wown[c] = summed(half)
+        wown[c][...] = summed(half)
 
     scale = ls_ref[...].reshape(1, D)
 
     def stage_four(c):
-        arrived(rs3.at[c], r_recv.at[c, 4])
-        cols = slice(c * COLS, c * COLS + COLS)
-        projected = wown[c] + rs3[c].astype(F32)
+        to_across(c).wait_recv()
+        cols = slice(STARTS[c], STARTS[c] + COLS[c])
+        projected = wown[c][...] + rs3[c][...].astype(F32)
         out_ref[:, cols] = (
             tok_ref[:, cols].astype(F32) + scale[:, cols] * projected
         ).astype(BF16)
@@ -467,16 +508,24 @@
         if 0 <= t - 1 < CHUNKS:
             stage_two(t - 1)
         if 0 <= t - 2 < CHUNKS:
-            stage_three(t - 2)
+            stage_relay(t - 2)
+        if 0 <= t - 3 < CHUNKS:
+            stage_three(t - 3)
     for c in range(CHUNKS):
         stage_four(c)
 
     sent(1)
     for c in range(CHUNKS):
         to_sibling(c).wait_send()
-        for dx in range(1, 4):
-            to_near(c, dx).wait_send()
+        for h in range(2):
+            far_copy(c, h).wait_send()
+            plain_copy(c, h).wait_send()
+            added_copy(c, h).wait_send()
         to_across(c).wait_send()
+
+
+def chunked(dtype, *dims):
+    return [pltpu.VMEM((*dims, cols), dtype) for cols in COLS]
 
 
 def shards(tokens, norm_gain, qkv_weight, q_gain, k_gain, out_weight, layer_scale):
@@ -500,21 +549,25 @@
             pltpu.VMEM((8, 8, 128), F32),
             pltpu.VMEM((8, 128), F32),
             pltpu.VMEM((8, 128), F32),
-            pltpu.VMEM((CHUNKS, 2, 256, COLS), BF16),
-            pltpu.VMEM((CHUNKS, 256, COLS), BF16),
-            pltpu.VMEM((CHUNKS, 4, 2, 32, COLS), BF16),
-            pltpu.VMEM((CHUNKS, 3, 2, 32, COLS), BF16),
-            pltpu.VMEM((CHUNKS, 32, COLS), F32),
-            pltpu.VMEM((CHUNKS, 32, COLS), BF16),
-            pltpu.VMEM((CHUNKS, 32, COLS), BF16),
+            *chunked(BF16, 2, 256),
+            *chunked(BF16, 256),
+            *chunked(BF16, 4, 2, 32),
+            *chunked(BF16, 2, 32),
+            *chunked(BF16, 2, 32),
+            *chunked(BF16, 2, 2, 32),
+            *chunked(F32, 32),
+            *chunked(BF16, 32),
+            *chunked(BF16, 32),
             dma((16, 2)),
             dma((15, 2)),
+            dma((5,)),
+            dma((5,)),
             dma((2, 32, 2)),
             dma((2, 6, 8, 2)),
             dma((9,)),
             dma((8,)),
-            dma((CHUNKS, 5)),
-            dma((CHUNKS, 5)),
+            dma((CHUNKS, 8)),
+            dma((CHUNKS, 8)),
         ],
         compiler_params=pltpu.CompilerParams(
             collective_id=0, has_side_effects=True, vmem_limit_bytes=60 * 1024 * 1024

time: 137 us -> 128 us (0.934)
  Pallas kernels: 134 us -> 125 us
    pallas_call x1, Pallas kernels: 134 us -> 125 us  [shards(): pl.pallas_call(kernel, out_shape=jax.ShapeDtypeStruct((32, D), BF16), in_...]
where the time goes in v3:
time: 128 us; the launch traced here: 127 us
  Pallas kernels  125 us (98%)
  local copies, waits for them, and re-layouts  1.62 us (1%)
    pallas_call x1, Pallas kernels, shards(): pl.pallas_call(kernel, out_shape=jax.ShapeDtypeStruct((32, D), BF16), in_...  125 us

profile of v3, /device:TPU:1, one launch (start us, length us, event | category | flops | bytes accessed | tf_op | source)
XLA Modules:
  0.0 127.0 jit_solution(2675980547523131043)
XLA Ops:
  0.0 125.4 %shard_map.73 = bf16[32,3200]{1,0:T(8,128)(2,1)} custom-call(bf16[32,3200]{1,0:T(8,128)(2,1)} %refs_0_.1, bf16[3200]{0:T(1024)(128)(2,1)} %refs_1_.1, bf16[3,100,256]{2,1,0:T(8,128)(2,1)} %refs_2_.1, bf16[100,256]{1,0:T(8,128)(2,1)} %bitcast.1, f32[256]{0:T(256)} %refs_4_.1, f32[256]{0:T(256)} %refs_5_.1, f32[3200]{0:T(1024)} %refs_6_.1), custom_call_target="tpu_custom_call" | custom-call | flops 4000000000 | bytes 1000000 | tf_op jit(solution)/shard_map/pallas_call | solution.py:534
  125.4 1.6 %copy.9 = bf16[32,3200]{1,0:T(8,128)(2,1)} copy(bf16[32,3200]{1,0:T(8,128)(2,1)} %shard_map.73) | data formatting | bytes 409600

commit v4 on v3

--- a/solution.py
+++ b/solution.py
@@ -12,7 +12,7 @@
 WIDTH = HEADS * HD
 QKV_ROWS = 304
 OUT_ROWS = 112
-COLS = (256, 512, 512, 640, 512, 512, 256)
+COLS = (640, 640, 640, 640, 640)
 CHUNKS = len(COLS)
 STARTS = tuple(sum(COLS[:c]) for c in range(CHUNKS))
 MESH = pl.DeviceIdType.MESH

time: 128 us -> 127 us (level)
  no operation moved by 1% of the time
where the time goes in v4:
time: 127 us
  Pallas kernels  125 us (98%)
  local copies, waits for them, and re-layouts  1.62 us (1%)
    pallas_call x1, Pallas kernels, shards(): pl.pallas_call(kernel, out_shape=jax.ShapeDtypeStruct((32, D), BF16), in_...  125 us

profile of v4, /device:TPU:1, one launch (start us, length us, event | category | flops | bytes accessed | tf_op | source)
XLA Modules:
  0.0 126.9 jit_solution(16578266526050624776)
XLA Ops:
  0.0 125.3 %shard_map.73 = bf16[32,3200]{1,0:T(8,128)(2,1)} custom-call(bf16[32,3200]{1,0:T(8,128)(2,1)} %refs_0_.1, bf16[3200]{0:T(1024)(128)(2,1)} %refs_1_.1, bf16[3,100,256]{2,1,0:T(8,128)(2,1)} %refs_2_.1, bf16[100,256]{1,0:T(8,128)(2,1)} %bitcast.1, f32[256]{0:T(256)} %refs_4_.1, f32[256]{0:T(256)} %refs_5_.1, f32[3200]{0:T(1024)} %refs_6_.1), custom_call_target="tpu_custom_call" | custom-call | flops 4000000000 | bytes 1000000 | tf_op jit(solution)/shard_map/pallas_call | solution.py:534
  125.3 1.6 %copy.9 = bf16[32,3200]{1,0:T(8,128)(2,1)} copy(bf16[32,3200]{1,0:T(8,128)(2,1)} %shard_map.73) | data formatting | bytes 409600

commit v5 on v4

--- a/solution.py
+++ b/solution.py
@@ -406,13 +406,6 @@
                 probs, heads[2, :, cols], preferred_element_type=F32
             ).astype(BF16)
 
-    for k in range(5):
-        z8_copy(k).wait_send()
-    for slot in range(1, 15):
-        for p in range(2):
-            tok_copy(half, x, core, p, sibling, slot).wait_send()
-    sent(0)
-
     @pl.loop(0, 8)
     def _(zs):
         finish(1, zs)
@@ -511,9 +504,12 @@
             stage_relay(t - 2)
         if 0 <= t - 3 < CHUNKS:
             stage_three(t - 3)
-    for c in range(CHUNKS):
-        stage_four(c)
-
+    for k in range(5):
+        z8_copy(k).wait_send()
+    for slot in range(1, 15):
+        for p in range(2):
+            tok_copy(half, x, core, p, sibling, slot).wait_send()
+    sent(0)
     sent(1)
     for c in range(CHUNKS):
         to_sibling(c).wait_send()
@@ -521,6 +517,11 @@
             far_copy(c, h).wait_send()
             plain_copy(c, h).wait_send()
             added_copy(c, h).wait_send()
+
+    for c in range(CHUNKS):
+        stage_four(c)
+
+    for c in range(CHUNKS):
         to_across(c).wait_send()
 
 

time: 127 us -> 126 us (level)
  no operation moved by 1% of the time
where the time goes in v5:
time: 126 us
  Pallas kernels  125 us (99%)
  local copies, waits for them, and re-layouts  1.62 us (1%)
    pallas_call x1, Pallas kernels, shards(): pl.pallas_call(kernel, out_shape=jax.ShapeDtypeStruct((32, D), BF16), in_...  125 us

profile of v5, /device:TPU:1, one launch (start us, length us, event | category | flops | bytes accessed | tf_op | source)
XLA Modules:
  0.0 126.3 jit_solution(17417483451664334132)
XLA Ops:
  0.0 124.7 %shard_map.73 = bf16[32,3200]{1,0:T(8,128)(2,1)} custom-call(bf16[32,3200]{1,0:T(8,128)(2,1)} %refs_0_.1, bf16[3200]{0:T(1024)(128)(2,1)} %refs_1_.1, bf16[3,100,256]{2,1,0:T(8,128)(2,1)} %refs_2_.1, bf16[100,256]{1,0:T(8,128)(2,1)} %bitcast.1, f32[256]{0:T(256)} %refs_4_.1, f32[256]{0:T(256)} %refs_5_.1, f32[3200]{0:T(1024)} %refs_6_.1), custom_call_target="tpu_custom_call" | custom-call | flops 4000000000 | bytes 1000000 | tf_op jit(solution)/shard_map/pallas_call | solution.py:535
  124.7 1.6 %copy.9 = bf16[32,3200]{1,0:T(8,128)(2,1)} copy(bf16[32,3200]{1,0:T(8,128)(2,1)} %shard_map.73) | data formatting | bytes 409600

commit v6 on v5

--- a/solution.py
+++ b/solution.py
@@ -12,7 +12,7 @@
 WIDTH = HEADS * HD
 QKV_ROWS = 304
 OUT_ROWS = 112
-COLS = (640, 640, 640, 640, 640)
+COLS = (512, 640, 768, 768, 512)
 CHUNKS = len(COLS)
 STARTS = tuple(sum(COLS[:c]) for c in range(CHUNKS))
 MESH = pl.DeviceIdType.MESH

time: 126 us -> 127 us (level)
  no operation moved by 1% of the time
where the time goes in v6:
time: 127 us
  Pallas kernels  125 us (98%)
  local copies, waits for them, and re-layouts  1.62 us (1%)
    pallas_call x1, Pallas kernels, shards(): pl.pallas_call(kernel, out_shape=jax.ShapeDtypeStruct((32, D), BF16), in_...  125 us

profile of v6, /device:TPU:1, one launch (start us, length us, event | category | flops | bytes accessed | tf_op | source)
XLA Modules:
  0.0 127.1 jit_solution(13668273764085678745)
XLA Ops:
  0.0 125.4 %shard_map.73 = bf16[32,3200]{1,0:T(8,128)(2,1)} custom-call(bf16[32,3200]{1,0:T(8,128)(2,1)} %refs_0_.1, bf16[3200]{0:T(1024)(128)(2,1)} %refs_1_.1, bf16[3,100,256]{2,1,0:T(8,128)(2,1)} %refs_2_.1, bf16[100,256]{1,0:T(8,128)(2,1)} %bitcast.1, f32[256]{0:T(256)} %refs_4_.1, f32[256]{0:T(256)} %refs_5_.1, f32[3200]{0:T(1024)} %refs_6_.1), custom_call_target="tpu_custom_call" | custom-call | flops 4000000000 | bytes 1000000 | tf_op jit(solution)/shard_map/pallas_call | solution.py:535
  125.4 1.6 %copy.9 = bf16[32,3200]{1,0:T(8,128)(2,1)} copy(bf16[32,3200]{1,0:T(8,128)(2,1)} %shard_map.73) | data formatting | bytes 409600
